TPU v7x, 256 devices: a whole 4x4x8 slice. The times are simulated.
256 devices in a mesh: chan: 32 (over z_lo, x, core), tm: 8 (over z_hi, y).
Axes of the slice: x: 4, y: 4, z: 8 (z_hi: 2, z_lo: 4; z = z_hi * 4 + z_lo), core: 2. Of those that a mesh axis runs over, the one named last changes fastest.
Arguments:
- traces: float32 [4096, 32768], P('chan', 'tm'), may hold values from -6 to 6
- offsets: int32 [32], P('tm'), may hold values from 0 to 4095, as said below
Outputs:
- stacks: float32 [4, 32, 4096, 128], P(None, None, ('chan', 'tm'))
Inputs may be any that keep to these rules, and one draw needn't show every extreme that they name: `offsets`: every time segment but at most one has a window that starts in the last 1024 samples of its segment.
All inputs are finite; a program needn't handle non-finite values.
Results may differ from a plain program's by a relative error of at most 0.0019.
Values may be sent and summed in bfloat16 or wider, within the bound.
A program may use at most 128 MiB of HBM per device.

v0:
```python
import math

import jax
import jax.numpy as jnp
from jax import lax
from jax.sharding import PartitionSpec as P

NFFT = 2048
BAND = 64
WIN_DEV = 4
ROUNDS = 4
NB = 16


def from_behind(block, axis, distance):
    devices = range(lax.axis_size(axis))
    route = [(i - distance, i) for i in devices if i - distance in devices]
    return lax.ppermute(block, axis, route)


def passed_along(block, axis, distance):
    devices = range(lax.axis_size(axis))
    route = [((i - distance) % len(devices), i) for i in devices]
    return lax.ppermute(block, axis, route)


def fourier_table(length):
    positions = jnp.arange(length, dtype=jnp.int32)
    phase = positions[:, None] * positions[None, : length // 2] % length
    angle = phase.astype(jnp.float32) * (2.0 * math.pi / length)
    return jnp.concatenate([jnp.cos(angle), -jnp.sin(angle)], axis=1)


def band_layout(whitened):
    channels = whitened.shape[0]
    moved = jnp.transpose(whitened, (3, 0, 1, 2, 4))
    return moved.reshape(NB, channels, -1)


def per_device(traces, offsets):
    channels = traces.shape[0]
    incoming = from_behind(traces[:, :NFFT], "tm", -1)
    extended = jnp.concatenate([traces, incoming], axis=1)
    pieces = []
    for window_index in range(WIN_DEV):
        pieces.append(lax.dynamic_slice_in_dim(extended, offsets[window_index], NFFT, 1))
    segments = jnp.stack(pieces, axis=1)
    centered = segments - jnp.mean(segments, axis=2, keepdims=True)
    normalized = centered * lax.rsqrt(jnp.mean(centered * centered, axis=2, keepdims=True) + 1e-06)
    spectrum = jnp.dot(
        normalized.reshape(-1, NFFT),
        fourier_table(NFFT),
        precision=lax.Precision.HIGHEST,
        preferred_element_type=jnp.float32,
    )
    real_part = spectrum[:, : NFFT // 2].reshape(-1, NB, BAND)
    imag_part = spectrum[:, NFFT // 2 :].reshape(-1, NB, BAND)
    magnitude = jnp.sqrt(real_part * real_part + imag_part * imag_part)
    factor = 1.0 / (jnp.mean(magnitude, axis=2, keepdims=True) + 1e-06)
    white_real = (real_part * factor).astype(jnp.bfloat16).reshape(channels, WIN_DEV, NB, BAND)
    white_imag = (imag_part * factor).astype(jnp.bfloat16).reshape(channels, WIN_DEV, NB, BAND)
    own_bands = band_layout(jnp.stack([white_real, white_imag], axis=2))
    norm_factor = 1.0 / math.sqrt(lax.axis_size("tm") * WIN_DEV * BAND)
    turned = band_layout(jnp.stack([white_imag, -white_real], axis=2))
    local_bands = own_bands.shape[0]
    results = []
    current = own_bands
    for which_round in range(ROUNDS):
        current = passed_along(own_bands, "chan", which_round + 1)
        real_sum = jnp.einsum(
            "bik,bjk->bij", own_bands, current, preferred_element_type=jnp.float32
        )
        imag_sum = jnp.einsum("bik,bjk->bij", turned, current, preferred_element_type=jnp.float32)
        terms = jnp.stack([real_sum, imag_sum], axis=0) * norm_factor
        results.append(terms.reshape(2 * local_bands, channels, channels))
    return lax.psum_scatter(jnp.stack(results), "tm", scatter_dimension=2, tiled=True)


def solution(mesh):
    return jax.shard_map(
        per_device,
        mesh=mesh,
        in_specs=(P("chan", "tm"), P("tm")),
        out_specs=P(None, None, ("chan", "tm"), None),
        check_vma=False,
    )
```

profile of v0, /device:TPU:65, one launch (start us, length us, event | category | flops | bytes accessed | tf_op | source)
XLA Modules:
  0.0 514.2 jit_solution(1125259352573203151)
XLA Ops:
  6.5 2.3 slice.26
  8.8 1.3 collective-permute-start
  10.1 0.7 fusion.19
  15.9 1.7 constant_dynamic-update-slice_fusion.1
  20.2 34.6 %fusion.10 = (f32[2048,1024]{1,0:T(8,128)}, f32[2048,1024]{1,0:T(8,128)}) fusion(s32[1024]{0:T(1024)S(1)} %iota_add_fusion), kind=kLoop, calls=%fused_computation.20 | loop fusion | flops 31457280 | bytes 16781312 | tf_op jit(solution)/shard_map/cos | solution.py:31
  54.9 1.3 constant_dynamic-update-slice_fusion
  56.2 1.2 constant_dynamic-slice_fusion.3
  57.3 0.7 stack.63
  58.1 0.7 stack.66
  58.8 0.7 stack.65
  59.5 0.7 stack.64
  60.3 6.8 %fusion.17 = (f32[128,4]{1,0:T(8,128)S(1)}, f32[128,4,2048]{2,1,0:T(4,128)}) fusion(f32[128,1,2048]{2,1,0:T(1,128)S(1)} %stack.66, f32[128,1,2048]{2,1,0:T(1,128)S(1)} %stack.65, f32[128,1,2048]{2,1,0:T(1,128)S(1)} %stack.64, f32[128,1,2048]{2,1,0:T(1,128)S(1)} %stack.63), kind=kLoop, calls=%fused_computation.52 | loop fusion | flops 4193792 | bytes 8390656 | tf_op jit(solution)/shard_map/reduce_sum | solution.py:48
  67.2 3.4 multiply_reduce_fusion
  70.6 5.3 %stack.68 = f32[512,2048]{1,0:T(8,128)} reshape(f32[128,4,2048]{2,1,0:T(4,128)} %get-tuple-element.8) | data formatting | bytes 8388608 | tf_op jit(solution)/shard_map/stack | solution.py:47
  76.0 33.3 %fusion = f32[512,2048]{1,0:T(8,128)S(1)} fusion(f32[2048,1024]{1,0:T(8,128)} %get-tuple-element.19, f32[2048,1024]{1,0:T(8,128)} %get-tuple-element.18, f32[512,2048]{1,0:T(8,128)} %stack.68, f32[512]{0:T(512)S(1)} %rsqrt.12, f32[512]{0:T(512)S(1)} %div.29), kind=kOutput, calls=%fused_computation | convolution fusion | flops 25776095232 | bytes 25169920 | tf_op jit(solution)/shard_map/dot_general | solution.py:50
  109.3 3.0 fusion.18
  112.3 4.5 reshape.149
  116.8 2.9 copy.36
  119.7 1.9 bitcast_reduce_fusion
  121.8 2.6 reshape.148
  124.3 3.0 multiply_convert_fusion
  127.3 0.4 copy-done.1
  127.8 1.4 fusion.16
  129.2 3.8 maximum_bitcast_fusion
  133.1 5.1 copy.38
  138.2 2.6 copy.39
  140.8 2.7 collective-permute-start.4
  143.5 2.4 collective-permute-start.3
  145.9 1.2 collective-permute-start.2
  147.2 5.9 %copy.41 = bf16[16,128,4,2,64]{1,4,3,2,0:T(8,128)(2,1)} copy(bf16[16,128,4,2,64]{4,0,2,1,3:T(8,128)(2,1)} %get-tuple-element.17) | data formatting | bytes 4194304 | tf_op jit(solution)/shard_map/transpose | solution.py:36
  153.1 36.9 %collective-permute-done.4 = bf16[16,128,512]{2,1,0:T(8,128)(2,1)} collective-permute-done((bf16[16,128,512]{2,1,0:T(8,128)(2,1)}, bf16[16,128,512]{2,1,0:T(8,128)(2,1)}, u32[]{:S(2)}, u32[]{:S(2)}) %collective-permute-start.4) | collective-permute-done | bytes 2097184 | tf_op jit(solution)/shard_map/ppermute | solution.py:24
  190.0 2.3 convolution_bitcast_fusion.1
  192.4 2.4 convolution_bitcast_fusion
  194.8 0.3 maximum_multiply_fusion.3
  195.1 46.0 %collective-permute-done.3 = bf16[16,128,512]{2,1,0:T(8,128)(2,1)} collective-permute-done((bf16[16,128,512]{2,1,0:T(8,128)(2,1)}, bf16[16,128,512]{2,1,0:T(8,128)(2,1)}, u32[]{:S(2)}, u32[]{:S(2)}) %collective-permute-start.3) | collective-permute-done | bytes 2097184 | tf_op jit(solution)/shard_map/ppermute | solution.py:24
  241.1 2.4 convolution_bitcast_fusion.2
  243.5 2.4 convolution_bitcast_fusion.3
  245.8 0.3 maximum_multiply_fusion.2
  246.1 37.9 %collective-permute-done.2 = bf16[16,128,512]{2,1,0:T(8,128)(2,1)} collective-permute-done((bf16[16,128,512]{2,1,0:T(8,128)(2,1)}, bf16[16,128,512]{2,1,0:T(8,128)(2,1)}, u32[]{:S(2)}, u32[]{:S(2)}) %collective-permute-start.2) | collective-permute-done | bytes 2097184 | tf_op jit(solution)/shard_map/ppermute | solution.py:24
  284.0 2.4 convolution_bitcast_fusion.4
  286.4 2.4 convolution_bitcast_fusion.5
  288.8 0.3 maximum_multiply_fusion.1
  289.1 12.6 %collective-permute-done.1 = bf16[16,128,512]{2,1,0:T(8,128)(2,1)} collective-permute-done((bf16[16,128,512]{2,1,0:T(8,128)(2,1)}, bf16[16,128,512]{2,1,0:T(8,128)(2,1)}, u32[]{:S(2)}, u32[]{:S(2)}) %collective-permute-start.1) | collective-permute-done | bytes 2097184 | tf_op jit(solution)/shard_map/ppermute | solution.py:24
  301.7 2.4 convolution_bitcast_fusion.6
  304.1 2.4 convolution_bitcast_fusion.7
  306.4 0.3 maximum_multiply_fusion
  306.7 3.8 pad_maximum_fusion
  310.5 196.9 %reduce-scatter.2.cloned.1.call-done = f32[4,32,16,128]{3,2,1,0:T(8,128)} async-done(((f32[4,32,128,128]{3,2,1,0:T(8,128)}), f32[4,32,16,128]{3,2,1,0:T(8,128)}) %reduce-scatter.2.cloned.1.call-update) | async-done | bytes 1048592 | tf_op jit(solution)/shard_map/reduce_scatter | solution.py:76
  (16 shorter events, 0.4 us)
Async XLA Ops:
  6.5 3.6 copy-start.2
  6.5 500.8 %reduce-scatter.2.cloned.1.call-start = ((), (), s32[]{:S(2)}) async-start(), calls=%async_computation.1 | async-start | bytes 9437184 | tf_op jit(solution)/shard_map/reduce_scatter | solution.py:76
  8.8 46.0 %collective-permute-start = (f32[128,2048]{1,0:T(8,128)}, f32[128,2048]{1,0:T(8,128)}, u32[]{:S(2)}, u32[]{:S(2)}) collective-permute-start(f32[128,2048]{1,0:T(8,128)} %slice.26), channel_id=1, source_target_pairs={{1,0},{2,1},{3,2},{4,3},{5,4},{6,5},{7,6},{9,8},{10,9},{11,10},{12... | collective-permute-start | bytes 3145736 | tf_op jit(solution)/shard_map/ppermute | solution.py:18
  124.3 3.4 copy-start.1
  140.8 49.3 %collective-permute-start.4 = (bf16[16,128,512]{2,1,0:T(8,128)(2,1)}, bf16[16,128,512]{2,1,0:T(8,128)(2,1)}, u32[]{:S(2)}, u32[]{:S(2)}) collective-permute-start(bf16[16,128,512]{2,1,0:T(8,128)(2,1)} %copy.39), channel_id=1, source_target_pairs={{224,0},{232,8},{240,16},{248,24},{0,32},{8,40},{16,48},{24,56},{3... | collective-permute-start | bytes 6291464 | tf_op jit(solution)/shard_map/ppermute | solution.py:24
  143.5 97.6 %collective-permute-start.3 = (bf16[16,128,512]{2,1,0:T(8,128)(2,1)}, bf16[16,128,512]{2,1,0:T(8,128)(2,1)}, u32[]{:S(2)}, u32[]{:S(2)}) collective-permute-start(bf16[16,128,512]{2,1,0:T(8,128)(2,1)} %copy.39), channel_id=1, source_target_pairs={{232,0},{240,8},{248,16},{0,24},{8,32},{16,40},{24,48},{32,56},{40... | collective-permute-start | bytes 6291464 | tf_op jit(solution)/shard_map/ppermute | solution.py:24
  145.9 138.1 %collective-permute-start.2 = (bf16[16,128,512]{2,1,0:T(8,128)(2,1)}, bf16[16,128,512]{2,1,0:T(8,128)(2,1)}, u32[]{:S(2)}, u32[]{:S(2)}) collective-permute-start(bf16[16,128,512]{2,1,0:T(8,128)(2,1)} %copy.39), channel_id=1, source_target_pairs={{240,0},{248,8},{0,16},{8,24},{16,32},{24,40},{32,48},{40,56},{48,... | collective-permute-start | bytes 6291464 | tf_op jit(solution)/shard_map/ppermute | solution.py:24
  147.1 154.5 %collective-permute-start.1 = (bf16[16,128,512]{2,1,0:T(8,128)(2,1)}, bf16[16,128,512]{2,1,0:T(8,128)(2,1)}, u32[]{:S(2)}, u32[]{:S(2)}) collective-permute-start(bf16[16,128,512]{2,1,0:T(8,128)(2,1)} %copy.39), channel_id=1, source_target_pairs={{248,0},{0,8},{8,16},{16,24},{24,32},{32,40},{40,48},{48,56},{56,6... | collective-permute-start | bytes 6291464 | tf_op jit(solution)/shard_map/ppermute | solution.py:24
  153.1 39.3 %copy-start = (bf16[16,128,4,2,64]{1,4,3,2,0:T(8,128)(2,1)S(1)}, bf16[16,128,4,2,64]{1,4,3,2,0:T(8,128)(2,1)}, u32[]{:S(2)}) copy-start(bf16[16,128,4,2,64]{1,4,3,2,0:T(8,128)(2,1)} %copy.41) | copy-start | bytes 6291460
Sparse Core Ops, SparseCore 0:
  310.6 196.6 reduce-scatter.1
where the time goes:
time: 519 us; the launch traced here: 514 us
  waiting for transfers between devices  330 us (64%)
  other arithmetic  63 us (12%)
  matrix products  52.2 us (10%)
  local copies, waits for them, and re-layouts  39.7 us (8%)
  between operations  21.3 us (4%)
  starting transfers between devices  7.69 us (1%)
    reduce_scatter x1, waiting for transfers between devices, per_device(): lax.psum_scatter(jnp.stack(results), 'tm', scatter_dimension=2, tiled=True)  197 us
    ppermute x4, waiting for transfers between devices, passed_along(): return lax.ppermute(block, axis, route)  133 us
    cos x1, other arithmetic, fourier_table(): return jnp.concatenate([jnp.cos(angle), -jnp.sin(angle)], axis=1)  34.6 us
    dot_general x1, matrix products, per_device(): jnp.dot(normalized.reshape(-1, NFFT), fourier_table(NFFT), precision=lax....  33.3 us
    transpose x2, local copies, waits for them, and re-layouts, band_layout(): moved = jnp.transpose(whitened, (3, 0, 1, 2, 4))  11 us
  transfers between devices with their start and end apart: 6, of which 5 were waited for; matrix products, arithmetic and copies ran while one was open for 11% of the time, Pallas kernels for 0%

commit v1 on v0

v1 whole, which is shorter than its diff:
```python
import functools
import math

import jax
import jax.numpy as jnp
import numpy as np
from jax import lax
from jax.experimental import pallas as pl
from jax.experimental.pallas import tpu as pltpu
from jax.sharding import PartitionSpec as P

NFFT = 2048
HALF = 1024
BAND = 64
SEG = 4096
WIN = 4
ROUNDS = 4
NB = 16
CH = 128
WINDOWS = 32
MESH = pl.DeviceIdType.MESH


def fourier_tables():
    position = np.arange(HALF, dtype=np.int64)[:, None]
    inner = np.arange(BAND // 2, dtype=np.int64)
    tables = []
    for parity in range(2):
        bins, imag = [], []
        for group in range(NB // 2):
            first, second = (group, group + 8) if parity == 0 else (group + 8, group)
            for is_imag in (False, True):
                for band in (first, second):
                    bins.append(band * BAND + 2 * inner + parity)
                    imag.append(np.full(inner.shape, is_imag))
        bins, imag = np.concatenate(bins)[None, :], np.concatenate(imag)[None, :]
        angle = (position * bins % NFFT).astype(np.float64) * (2.0 * math.pi / NFFT)
        tables.append(np.where(imag, -np.sin(angle), np.cos(angle)))
    table = np.stack(tables)
    high = table.astype(jnp.bfloat16)
    low = (table - high.astype(np.float64)).astype(jnp.bfloat16)
    return np.stack([high, low])


def kernel(
    traces, offsets, tables, out,
    ext, tab, turns, split, white, rec, acc, own_out, far_out, own_in, far_in,
    load_sem, tab_sem, halo_send, halo_recv, b_send, b_recv, c_send, c_recv, d_send, d_recv, known,
):
    chan, tm = lax.axis_index("chan"), lax.axis_index("tm")
    zl, x, core = chan // 8, chan // 2 % 4, chan % 2
    zh, y = tm // 4, tm % 4
    block = chan % 8
    band = 4 * x + y
    plane = zl * 8
    sibling = (chan + 1 - 2 * core, tm)
    following = jnp.where(core == 0, chan + 1, (zl + 1) % 4 * 8 + 2 * x)
    preceding = jnp.where(core == 0, (zl + 3) % 4 * 8 + 2 * x + 1, chan - 1)

    load = pltpu.make_async_copy(traces, ext.at[:, pl.ds(0, SEG)], load_sem)
    load.start()
    table_load = pltpu.make_async_copy(tables, tab, tab_sem)
    table_load.start()

    def x_peer(step):
        return (plane + (x + step) % 4 * 2 + core, tm)

    def y_peer(step):
        return (chan, zh * 4 + (y + step) % 4)

    partner = (chan, (1 - zh) * 4 + y)

    barrier = pltpu.get_barrier_semaphore()
    for step in range(1, 4):
        pl.semaphore_signal(barrier, inc=1, device_id=x_peer(step), device_id_type=MESH)
        pl.semaphore_signal(barrier, inc=1, device_id=y_peer(step), device_id_type=MESH)
    pl.semaphore_signal(barrier, inc=1, device_id=sibling, device_id_type=MESH)
    pl.semaphore_signal(barrier, inc=1, device_id=partner, device_id_type=MESH)
    pl.semaphore_signal(barrier, inc=1, device_id=(following, tm), device_id_type=MESH)
    pl.semaphore_signal(barrier, inc=1, device_id=(preceding, tm), device_id_type=MESH)

    @pl.when(tm == 4)
    def _():
        pl.semaphore_signal(barrier, inc=1, device_id=(chan, tm - 1), device_id_type=MESH)

    @pl.when(tm == 3)
    def _():
        pl.semaphore_signal(barrier, inc=1, device_id=(chan, tm + 1), device_id_type=MESH)

    at_fold = jnp.logical_or(tm == 3, tm == 4)

    @pl.when(at_fold)
    def _():
        pl.semaphore_wait(barrier, 11)

    @pl.when(jnp.logical_not(at_fold))
    def _():
        pl.semaphore_wait(barrier, 10)

    halo = pltpu.make_async_remote_copy(
        src_ref=traces.at[:, pl.ds(0, NFFT)],
        dst_ref=ext.at[:, pl.ds(SEG, NFFT)],
        send_sem=halo_send,
        recv_sem=halo_recv,
        device_id=(chan, jnp.maximum(tm - 1, 0)),
        device_id_type=MESH,
    )

    @pl.when(tm > 0)
    def _():
        halo.start()

    for step in range(1, 4):
        pl.semaphore_signal(known.at[0], inc=1, device_id=y_peer(step), device_id_type=MESH)
    pl.semaphore_wait(known.at[0], 3)
    pl.semaphore_signal(known.at[1], inc=1, device_id=sibling, device_id_type=MESH)
    pl.semaphore_wait(known.at[1], 1)
    pl.semaphore_signal(known.at[2], inc=1, device_id=partner, device_id_type=MESH)
    pl.semaphore_wait(known.at[2], 1)

    @pl.when(tm == 7)
    def _():
        ext[:, pl.ds(SEG, NFFT)] = jnp.zeros((CH, NFFT), jnp.float32)

    column = lax.broadcasted_iota(jnp.int32, (NB, 128), 1)
    row = lax.broadcasted_iota(jnp.int32, (NB, 128), 0)
    swapped = row // 8
    frequency = row * BAND + 2 * (column % 32) + (column // 32 + swapped) % 2
    for w in range(WIN):
        angle = (frequency * offsets[w] % NFFT).astype(jnp.float32) * (2.0 * math.pi / NFFT)
        turns[w, 0] = jnp.cos(angle)
        turns[w, 1] = jnp.where(column < 64, -1.0, 1.0) * jnp.sin(angle)

    load.wait()
    table_load.wait()

    @pl.when(tm < 7)
    def _():
        halo.wait_recv()

    lane = lax.broadcasted_iota(jnp.int32, (CH, 128), 1)
    even_quarter = lane // 32 % 2 == 0
    to_mine = block // 4 == core

    def b_copy(w, dx, dy):
        to_x, to_y = (x + dx) % 4, (y + dy) % 4
        return pltpu.make_async_remote_copy(
            src_ref=white.at[w, to_x * 4 + to_y],
            dst_ref=rec.at[w, y, 4 + block % 4],
            send_sem=b_send.at[w, dx * 4 + dy],
            recv_sem=b_recv.at[w, y, block % 4],
            device_id=(plane + to_x * 2 + block // 4, zh * 4 + to_y),
            device_id_type=MESH,
        )

    def transform(w, carry):
        start = offsets[w]
        parts = []
        for k in range(16):
            place = lane + 128 * k
            near, middle, far = (ext[:, pl.ds(NFFT * part + 128 * k, 128)] for part in range(3))
            parts.append(jnp.where(place >= start, near, jnp.where(place >= start - NFFT, middle, far)))
        mean = jnp.sum(functools.reduce(jnp.add, parts), axis=1, keepdims=True) * (1.0 / NFFT)
        parts = [part - mean for part in parts]
        power = jnp.sum(functools.reduce(jnp.add, [part * part for part in parts]), axis=1, keepdims=True)
        scale = lax.rsqrt(power * (1.0 / NFFT) + 1e-06)
        parts = [part * scale for part in parts]
        for k in range(8):
            for parity in range(2):
                value = parts[k] + parts[k + 8] if parity == 0 else parts[k] - parts[k + 8]
                high = value.astype(jnp.bfloat16)
                split[parity, pl.ds(0, CH), pl.ds(128 * k, 128)] = high
                split[parity, pl.ds(CH, CH), pl.ds(128 * k, 128)] = (value - high.astype(jnp.float32)).astype(jnp.bfloat16)
        for quarter in range(4):
            columns = pl.ds(256 * quarter, 256)
            both = []
            for parity in range(2):
                main = jnp.dot(split[parity], tab[0, parity, :, columns], preferred_element_type=jnp.float32)
                rest = jnp.dot(split[parity, pl.ds(0, CH), :], tab[1, parity, :, columns], preferred_element_type=jnp.float32)
                both.append(main[:CH] + main[CH:] + rest)
            for group in range(2):
                j = 2 * quarter + group
                even, odd = (part[:, 128 * group : 128 * group + 128] for part in both)
                for which, tile in ((j, jnp.where(even_quarter, even, odd)), (j + 8, jnp.where(even_quarter, odd, even))):
                    square = tile * tile
                    size = jnp.sqrt(square + pltpu.roll(square, 64, 1))
                    level = jnp.sum(size, axis=1, keepdims=True) * (0.5 / BAND)
                    tile = tile * (1.0 / (level + 1e-06))
                    straight = turns[w, 0, which : which + 1, :]
                    across = turns[w, 1, which : which + 1, :]
                    white[w, which] = (tile * straight + pltpu.roll(tile, 64, 1) * across).astype(jnp.bfloat16)
        for dx in range(4):
            for dy in range(4):
                if dx == 0 and dy == 0:

                    @pl.when(to_mine)
                    def _():
                        rec[w, y, 4 + block % 4] = white[w, band]

                    @pl.when(jnp.logical_not(to_mine))
                    def _():
                        b_copy(w, 0, 0).start()
                else:
                    b_copy(w, dx, dy).start()
        return carry

    lax.fori_loop(0, WIN, transform, 0)

    def c_copy(w, from_y):
        return pltpu.make_async_remote_copy(
            src_ref=rec.at[w, from_y, pl.ds(4, 4)],
            dst_ref=rec.at[w, from_y, pl.ds(0, 4)],
            send_sem=c_send.at[w, from_y],
            recv_sem=c_recv.at[w, from_y],
            device_id=(following, tm),
            device_id_type=MESH,
        )

    def forward(w):
        for from_y in range(4):
            for i in range(4):
                arrival = pltpu.make_async_remote_copy(
                    src_ref=white.at[w, 0],
                    dst_ref=rec.at[w, from_y, 4 + i],
                    send_sem=b_send.at[w, 0],
                    recv_sem=b_recv.at[w, from_y, i],
                    device_id=sibling,
                    device_id_type=MESH,
                )
                mine = jnp.logical_and(block == 4 * core + i, y == from_y)

                @pl.when(jnp.logical_not(mine))
                def _():
                    arrival.wait_recv()

            c_copy(w, from_y).start()

    sign = jnp.where(lane < 64, 1.0, -1.0)

    def cross(w, i):
        own = [rec[w, from_y, 4 + i] for from_y in range(4)]
        turned = [(pltpu.roll(tile.astype(jnp.float32), 64, 1) * sign).astype(jnp.bfloat16) for tile in own]
        left = jnp.concatenate([jnp.concatenate(own, axis=1), jnp.concatenate(turned, axis=1)], axis=0)
        right = jnp.concatenate([rec[w, from_y, pl.ds(i, 4)].reshape(4 * CH, 128) for from_y in range(4)], axis=1)
        return lax.dot_general(left, right, (((1,), (1,)), ((), ())), preferred_element_type=jnp.float32)

    def add_window(w):
        for from_y in range(4):
            c_copy(w, from_y).wait_recv()

        def one(i, carry):
            @pl.when(w == 0)
            def _():
                acc[i] = cross(w, i)

            @pl.when(w > 0)
            def _():
                acc[i] += cross(w, i)

            return carry

        lax.fori_loop(0, 4, one, 0)

    def exchange(w, carry):
        forward(w)

        @pl.when(w > 0)
        def _():
            add_window(w - 1)

        return carry

    lax.fori_loop(0, WIN, exchange, 0)
    for from_y in range(4):
        c_copy(WIN - 1, from_y).wait_recv()

    norm = 1.0 / math.sqrt(WINDOWS * BAND)

    def far_copy(i, dy):
        to_y = (y + dy) % 4
        return pltpu.make_async_remote_copy(
            src_ref=far_out.at[i, to_y],
            dst_ref=far_in.at[band],
            send_sem=d_send.at[0, i, dy],
            recv_sem=d_recv.at[0, band],
            device_id=(plane + 4 * core + i, (1 - zh) * 4 + to_y),
            device_id_type=MESH,
        )

    def own_copy(i, dy):
        to_y = (y + dy) % 4
        return pltpu.make_async_remote_copy(
            src_ref=own_out.at[i, to_y],
            dst_ref=own_in.at[band],
            send_sem=d_send.at[1, i, dy],
            recv_sem=d_recv.at[1, band],
            device_id=(plane + 4 * core + i, zh * 4 + to_y),
            device_id_type=MESH,
        )

    def give(step, carry):
        i = (step + x) % 4
        acc[i] = (acc[i] + cross(WIN - 1, i)) * norm
        for to_y in range(4):
            for r in range(ROUNDS):
                for part in range(2):
                    columns = pl.ds(128 * (ROUNDS - 1 - r), 128)
                    far_rows = pl.ds(pl.multiple_of(part * CH + 64 * (1 - zh) + 16 * to_y, 16), 16)
                    far_out[i, to_y, r, part] = acc[i, far_rows, columns].astype(jnp.bfloat16)
                    own_rows = pl.ds(pl.multiple_of(part * CH + 64 * zh + 16 * to_y, 16), 16)
                    own_out[i, to_y, r, part] = acc[i, own_rows, columns]
        for dy in range(4):
            far_copy(i, dy).start()
        for dy in range(4):
            if dy == 0:
                mine = block == 4 * core + i

                @pl.when(mine)
                def _():
                    own_in[band] = own_out[i, y]

                @pl.when(jnp.logical_not(mine))
                def _():
                    own_copy(i, 0).start()
            else:
                own_copy(i, dy).start()
        return carry

    lax.fori_loop(0, 4, give, 0)

    def take(m, carry):
        arrival = pltpu.make_async_remote_copy(
            src_ref=own_out.at[0, 0], dst_ref=own_in.at[m], send_sem=d_send.at[1, 0, 0],
            recv_sem=d_recv.at[1, m], device_id=sibling, device_id_type=MESH,
        )
        mine = jnp.logical_and(m == band, to_mine)

        @pl.when(jnp.logical_not(mine))
        def _():
            arrival.wait_recv()

        pltpu.make_async_remote_copy(
            src_ref=far_out.at[0, 0], dst_ref=far_in.at[m], send_sem=d_send.at[0, 0, 0],
            recv_sem=d_recv.at[0, m], device_id=sibling, device_id_type=MESH,
        ).wait_recv()
        for r in range(ROUNDS):
            for part in range(2):
                out[r, part * NB + m] = own_in[m, r, part] + far_in[m, r, part].astype(jnp.float32)
        return carry

    lax.fori_loop(0, NB, take, 0)

    @pl.when(tm > 0)
    def _():
        halo.wait_send()

    def b_left(w, carry):
        for dx in range(4):
            for dy in range(4):
                if dx == 0 and dy == 0:

                    @pl.when(jnp.logical_not(to_mine))
                    def _():
                        b_copy(w, 0, 0).wait_send()
                else:
                    b_copy(w, dx, dy).wait_send()
        for from_y in range(4):
            c_copy(w, from_y).wait_send()
        return carry

    lax.fori_loop(0, WIN, b_left, 0)

    def d_left(i, carry):
        for dy in range(4):
            far_copy(i, dy).wait_send()
            if dy == 0:

                @pl.when(block != 4 * core + i)
                def _():
                    own_copy(i, 0).wait_send()
            else:
                own_copy(i, dy).wait_send()
        return carry

    lax.fori_loop(0, 4, d_left, 0)


def per_device(traces, offsets):
    tables = jnp.asarray(fourier_tables())
    dma = pltpu.SemaphoreType.DMA
    piece = (ROUNDS, 2, 16, CH)
    return pl.pallas_call(
        kernel,
        out_shape=jax.ShapeDtypeStruct((ROUNDS, 2 * NB, 16, CH), jnp.float32),
        in_specs=[
            pl.BlockSpec(memory_space=pl.ANY),
            pl.BlockSpec(memory_space=pltpu.SMEM),
            pl.BlockSpec(memory_space=pl.ANY),
        ],
        out_specs=pl.BlockSpec(memory_space=pltpu.VMEM),
        scratch_shapes=[
            pltpu.VMEM((CH, SEG + NFFT), jnp.float32),
            pltpu.VMEM((2, 2, HALF, HALF), jnp.bfloat16),
            pltpu.VMEM((WIN, 2, NB, 128), jnp.float32),
            pltpu.VMEM((2, 2 * CH, HALF), jnp.bfloat16),
            pltpu.VMEM((WIN, NB, CH, 128), jnp.bfloat16),
            pltpu.VMEM((WIN, 4, 8, CH, 128), jnp.bfloat16),
            pltpu.VMEM((4, 2 * CH, ROUNDS * CH), jnp.float32),
            pltpu.VMEM((4, 4) + piece, jnp.float32),
            pltpu.VMEM((4, 4) + piece, jnp.bfloat16),
            pltpu.VMEM((NB,) + piece, jnp.float32),
            pltpu.VMEM((NB,) + piece, jnp.bfloat16),
            dma, dma, dma, dma,
            dma((WIN, 16)), dma((WIN, 4, 4)), dma((WIN, 4)), dma((WIN, 4)), dma((2, 4, 4)), dma((2, NB)),
            pltpu.SemaphoreType.REGULAR((3,)),
        ],
        compiler_params=pltpu.CompilerParams(
            collective_id=0, has_side_effects=True, vmem_limit_bytes=48 * 1024 * 1024
        ),
        cost_estimate=pl.CostEstimate(flops=8_000_000_000, bytes_accessed=16_000_000, transcendentals=1_000_000),
    )(traces, offsets, tables)


def solution(mesh):
    return jax.shard_map(
        per_device,
        mesh=mesh,
        in_specs=(P("chan", "tm"), P("tm")),
        out_specs=P(None, None, ("chan", "tm"), None),
        check_vma=False,
    )
```

time: 519 us -> 154 us (0.30)
  waiting for transfers between devices: 330 us -> 0 us
  Pallas kernels: 0 us -> 150 us
  other arithmetic: 63 us -> 0 us
  matrix products: 52.2 us -> 0 us
  local copies, waits for them, and re-layouts: 39.7 us -> 3.22 us
  between operations: 21.3 us -> 0.01 us
  starting transfers between devices: 7.69 us -> 0 us
    reduce_scatter x1 -> x0, waiting for transfers between devices: 197 us -> none  [per_device(): lax.psum_scatter(jnp.stack(results), 'tm', scatter_dimension=2, tiled=True)]
    pallas_call x0 -> x1, Pallas kernels: none -> 150 us  [per_device(): pl.pallas_call(kernel, out_shape=jax.ShapeDtypeStruct((ROUNDS, 2 * NB, 16...]
    ppermute x5 -> x0, waiting for transfers between devices: 133 us -> none  [the longest x4 133 us: passed_along(): return lax.ppermute(block, axis, route)]
    dot_general x9 -> x0, matrix products: 52.2 us -> none  [the longest x1 33.3 us: per_device(): jnp.dot(normalized.reshape(-1, NFFT), fourier_table(NFFT), precision=lax....]
    cos x1 -> x0, other arithmetic: 34.6 us -> none  [fourier_table(): return jnp.concatenate([jnp.cos(angle), -jnp.sin(angle)], axis=1)]
    reduce_sum x3 -> x0, other arithmetic: 12.1 us -> none  [the longest x1 6.82 us: per_device(): centered = segments - jnp.mean(segments, axis=2, keepdims=True)]
    transpose x2 -> x0, local copies, waits for them, and re-layouts: 11 us -> none  [band_layout(): moved = jnp.transpose(whitened, (3, 0, 1, 2, 4))]
    reshape x3 -> x0, local copies, waits for them, and re-layouts: 9.67 us -> none  [the longest x1 4.51 us: per_device(): imag_part = spectrum[:, NFFT // 2:].reshape(-1, NB, BAND)]
  transfers between devices with their start and end apart: 6 -> 0, of which waited for: 5 -> 0; matrix products, arithmetic and copies ran while one was open for 11% -> 0% of each run, Pallas kernels for 0% -> 0%
where the time goes in v1:
time: 154 us
  Pallas kernels  150 us (97%)
  local copies, waits for them, and re-layouts  3.22 us (2%)
    pallas_call x1, Pallas kernels, per_device(): pl.pallas_call(kernel, out_shape=jax.ShapeDtypeStruct((ROUNDS, 2 * NB, 16...  150 us
    unnamed x5, local copies, waits for them, and re-layouts  3.22 us

profile of v1, /device:TPU:65, one launch (start us, length us, event | category | flops | bytes accessed | tf_op | source)
XLA Modules:
  0.0 153.5 jit_solution(8166737897179714094)
XLA Ops:
  0.0 0.0 copy-start
  0.0 1.6 %copy-done = f32[128,4096]{1,0:T(8,128)S(1)} copy-done((f32[128,4096]{1,0:T(8,128)S(1)}, f32[128,4096]{1,0:T(8,128)}, u32[]{:S(2)}) %copy-start) | copy-done | bytes 2097176
  1.6 0.0 copy-start.1
  1.6 0.7 copy-done.1
  2.2 150.3 %shard_map.37 = f32[4,32,16,128]{3,2,1,0:T(8,128)S(1)} custom-call(f32[128,4096]{1,0:T(8,128)S(1)} %copy-done, s32[4]{0:T(128)S(1)} %copy-done.1, bf16[2,2,1024,1024]{3,2,1,0:T(8,128)(2,1)} %constant.2.clone.tables), custom_call_target="tpu_custom_call" | custom-call | flops 8000000000 | bytes 16000000 | tf_op jit(solution)/shard_map/pallas_call | solution.py:392
  152.5 1.0 copy.5
Async XLA Ops:
  0.0 1.6 %copy-start = (f32[128,4096]{1,0:T(8,128)S(1)}, f32[128,4096]{1,0:T(8,128)}, u32[]{:S(2)}) copy-start(f32[128,4096]{1,0:T(8,128)} %traces.1) | copy-start | bytes 6291460
  1.6 0.7 copy-start.1

commit v2 on v1

--- a/solution.py
+++ b/solution.py
@@ -19,6 +19,10 @@
 CH = 128
 WINDOWS = 32
 MESH = pl.DeviceIdType.MESH
+FOLD = ((4, 7, 3), (4, 0, 3), (4, 5, 1, 3), (4, 6, 2, 3))
+FAR_FIRST = (
+    (2, 2), (2, 0), (0, 2), (2, 1), (3, 2), (2, 3), (1, 2), (1, 1), (3, 3), (1, 3), (3, 1), (1, 0), (3, 0), (0, 1), (0, 3),
+)
 
 
 def fourier_tables():
@@ -45,7 +49,7 @@
 def kernel(
     traces, offsets, tables, out,
     ext, tab, turns, split, white, rec, acc, own_out, far_out, own_in, far_in,
-    load_sem, tab_sem, halo_send, halo_recv, b_send, b_recv, c_send, c_recv, d_send, d_recv, known,
+    relay, load_sem, tab_sem, halo_send, halo_recv, fold_send, fold_recv, b_send, b_recv, c_send, c_recv, d_send, d_recv, known,
 ):
     chan, tm = lax.axis_index("chan"), lax.axis_index("tm")
     zl, x, core = chan // 8, chan // 2 % 4, chan % 2
@@ -57,11 +61,6 @@
     following = jnp.where(core == 0, chan + 1, (zl + 1) % 4 * 8 + 2 * x)
     preceding = jnp.where(core == 0, (zl + 3) % 4 * 8 + 2 * x + 1, chan - 1)
 
-    load = pltpu.make_async_copy(traces, ext.at[:, pl.ds(0, SEG)], load_sem)
-    load.start()
-    table_load = pltpu.make_async_copy(tables, tab, tab_sem)
-    table_load.start()
-
     def x_peer(step):
         return (plane + (x + step) % 4 * 2 + core, tm)
 
@@ -79,23 +78,7 @@
     pl.semaphore_signal(barrier, inc=1, device_id=(following, tm), device_id_type=MESH)
     pl.semaphore_signal(barrier, inc=1, device_id=(preceding, tm), device_id_type=MESH)
 
-    @pl.when(tm == 4)
-    def _():
-        pl.semaphore_signal(barrier, inc=1, device_id=(chan, tm - 1), device_id_type=MESH)
-
-    @pl.when(tm == 3)
-    def _():
-        pl.semaphore_signal(barrier, inc=1, device_id=(chan, tm + 1), device_id_type=MESH)
-
-    at_fold = jnp.logical_or(tm == 3, tm == 4)
-
-    @pl.when(at_fold)
-    def _():
-        pl.semaphore_wait(barrier, 11)
-
-    @pl.when(jnp.logical_not(at_fold))
-    def _():
-        pl.semaphore_wait(barrier, 10)
+    pl.semaphore_wait(barrier, 10)
 
     halo = pltpu.make_async_remote_copy(
         src_ref=traces.at[:, pl.ds(0, NFFT)],
@@ -105,10 +88,35 @@
         device_id=(chan, jnp.maximum(tm - 1, 0)),
         device_id_type=MESH,
     )
-
-    @pl.when(tm > 0)
+    direct_out = jnp.logical_and(tm > 0, tm != 4)
+    direct_in = jnp.logical_and(tm < 7, tm != 3)
+
+    def fold_copy(way, piece, leg):
+        first, last = leg == 0, leg == len(FOLD[way]) - 2
+        rows = pl.ds(32 * way + 8 * piece, 8)
+        return pltpu.make_async_remote_copy(
+            src_ref=traces.at[rows, pl.ds(0, NFFT)] if first else relay.at[piece],
+            dst_ref=ext.at[rows, pl.ds(SEG, NFFT)] if last else relay.at[piece],
+            send_sem=fold_send.at[way, piece],
+            recv_sem=fold_recv.at[way, piece],
+            device_id=(chan, jnp.int32(FOLD[way][leg + 1])),
+            device_id_type=MESH,
+        )
+
+    @pl.when(direct_out)
     def _():
         halo.start()
+
+    @pl.when(tm == 4)
+    def _():
+        for piece in range(4):
+            for way in range(4):
+                fold_copy(way, piece, 0).start()
+
+    load = pltpu.make_async_copy(traces, ext.at[:, pl.ds(0, SEG)], load_sem)
+    load.start()
+    table_load = pltpu.make_async_copy(tables, tab, tab_sem)
+    table_load.start()
 
     for step in range(1, 4):
         pl.semaphore_signal(known.at[0], inc=1, device_id=y_peer(step), device_id_type=MESH)
@@ -134,9 +142,28 @@
     load.wait()
     table_load.wait()
 
-    @pl.when(tm < 7)
+    for way, path in enumerate(FOLD):
+        for leg in range(1, len(path) - 1):
+
+            @pl.when(tm == path[leg])
+            def _():
+                for piece in range(4):
+                    fold_copy(way, piece, leg - 1).wait_recv()
+                    fold_copy(way, piece, leg).start()
+
+    @pl.when(direct_in)
     def _():
         halo.wait_recv()
+
+    @pl.when(tm == 3)
+    def _():
+        for way, path in enumerate(FOLD):
+            for piece in range(4):
+                fold_copy(way, piece, len(path) - 2).wait_recv()
+
+    for step in range(1, 4):
+        pl.semaphore_signal(known.at[3], inc=1, device_id=y_peer(step), device_id_type=MESH)
+    pl.semaphore_wait(known.at[3], 3)
 
     lane = lax.broadcasted_iota(jnp.int32, (CH, 128), 1)
     even_quarter = lane // 32 % 2 == 0
@@ -189,19 +216,17 @@
                     straight = turns[w, 0, which : which + 1, :]
                     across = turns[w, 1, which : which + 1, :]
                     white[w, which] = (tile * straight + pltpu.roll(tile, 64, 1) * across).astype(jnp.bfloat16)
-        for dx in range(4):
-            for dy in range(4):
-                if dx == 0 and dy == 0:
-
-                    @pl.when(to_mine)
-                    def _():
-                        rec[w, y, 4 + block % 4] = white[w, band]
-
-                    @pl.when(jnp.logical_not(to_mine))
-                    def _():
-                        b_copy(w, 0, 0).start()
-                else:
-                    b_copy(w, dx, dy).start()
+        for dx, dy in FAR_FIRST:
+            b_copy(w, dx, dy).start()
+
+        @pl.when(to_mine)
+        def _():
+            rec[w, y, 4 + block % 4] = white[w, band]
+
+        @pl.when(jnp.logical_not(to_mine))
+        def _():
+            b_copy(w, 0, 0).start()
+
         return carry
 
     lax.fori_loop(0, WIN, transform, 0)
@@ -350,9 +375,17 @@
 
     lax.fori_loop(0, NB, take, 0)
 
-    @pl.when(tm > 0)
+    @pl.when(direct_out)
     def _():
         halo.wait_send()
+
+    for way, path in enumerate(FOLD):
+        for leg in range(len(path) - 1):
+
+            @pl.when(tm == path[leg])
+            def _():
+                for piece in range(4):
+                    fold_copy(way, piece, leg).wait_send()
 
     def b_left(w, carry):
         for dx in range(4):
@@ -410,12 +443,13 @@
             pltpu.VMEM((4, 4) + piece, jnp.bfloat16),
             pltpu.VMEM((NB,) + piece, jnp.float32),
             pltpu.VMEM((NB,) + piece, jnp.bfloat16),
-            dma, dma, dma, dma,
+            pltpu.VMEM((4, 8, NFFT), jnp.float32),
+            dma, dma, dma, dma, dma((4, 4)), dma((4, 4)),
             dma((WIN, 16)), dma((WIN, 4, 4)), dma((WIN, 4)), dma((WIN, 4)), dma((2, 4, 4)), dma((2, NB)),
-            pltpu.SemaphoreType.REGULAR((3,)),
+            pltpu.SemaphoreType.REGULAR((4,)),
         ],
         compiler_params=pltpu.CompilerParams(
-            collective_id=0, has_side_effects=True, vmem_limit_bytes=48 * 1024 * 1024
+            collective_id=0, has_side_effects=True, vmem_limit_bytes=60 * 1024 * 1024
         ),
         cost_estimate=pl.CostEstimate(flops=8_000_000_000, bytes_accessed=16_000_000, transcendentals=1_000_000),
     )(traces, offsets, tables)

time: 154 us -> 109 us (0.71)
  the two profiles are of different devices: /device:TPU:65 before, /device:TPU:129 now
where the time goes in v2:
time: 109 us
  Pallas kernels  107 us (98%)
  local copies, waits for them, and re-layouts  2.29 us (2%)
    pallas_call x1, Pallas kernels, per_device(): pl.pallas_call(kernel, out_shape=jax.ShapeDtypeStruct((ROUNDS, 2 * NB, 16...  107 us
    unnamed x1, local copies, waits for them, and re-layouts  2.29 us

profile of v2, /device:TPU:129, one launch (start us, length us, event | category | flops | bytes accessed | tf_op | source)
XLA Modules:
  0.0 109.3 jit_solution(7204945188101480587)
XLA Ops:
  0.0 107.1 %shard_map.37 = f32[4,32,16,128]{3,2,1,0:T(8,128)} custom-call(f32[128,4096]{1,0:T(8,128)} %traces.1, s32[4]{0:T(128)} %offsets.1, bf16[2,2,1024,1024]{3,2,1,0:T(8,128)(2,1)} %constant.2.clone.tables), custom_call_target="tpu_custom_call" | custom-call | flops 8000000000 | bytes 16000000 | tf_op jit(solution)/shard_map/pallas_call | solution.py:425
  107.1 2.3 %copy.5 = f32[4,32,16,128]{3,2,1,0:T(8,128)} copy(f32[4,32,16,128]{3,2,1,0:T(8,128)} %shard_map.37) | data formatting | bytes 2097152

commit v3 on v2

--- a/solution.py
+++ b/solution.py
@@ -19,7 +19,8 @@
 CH = 128
 WINDOWS = 32
 MESH = pl.DeviceIdType.MESH
-FOLD = ((4, 7, 3), (4, 0, 3), (4, 5, 1, 3), (4, 6, 2, 3))
+FOLD = (((4, 7, 3), range(0, 6)), ((4, 0, 3), range(6, 12)), ((4, 5, 1, 2, 3), range(12, 16)))
+FOLD_ORDER = (12, 0, 6, 13, 1, 7, 14, 2, 8, 15, 3, 9, 4, 10, 5, 11)
 FAR_FIRST = (
     (2, 2), (2, 0), (0, 2), (2, 1), (3, 2), (2, 3), (1, 2), (1, 1), (3, 3), (1, 3), (3, 1), (1, 0), (3, 0), (0, 1), (0, 3),
 )
@@ -91,15 +92,15 @@
     direct_out = jnp.logical_and(tm > 0, tm != 4)
     direct_in = jnp.logical_and(tm < 7, tm != 3)
 
-    def fold_copy(way, piece, leg):
-        first, last = leg == 0, leg == len(FOLD[way]) - 2
-        rows = pl.ds(32 * way + 8 * piece, 8)
+    def fold_copy(path, piece, leg):
+        first, last = leg == 0, leg == len(path) - 2
+        rows = pl.ds(8 * piece, 8)
         return pltpu.make_async_remote_copy(
             src_ref=traces.at[rows, pl.ds(0, NFFT)] if first else relay.at[piece],
             dst_ref=ext.at[rows, pl.ds(SEG, NFFT)] if last else relay.at[piece],
-            send_sem=fold_send.at[way, piece],
-            recv_sem=fold_recv.at[way, piece],
-            device_id=(chan, jnp.int32(FOLD[way][leg + 1])),
+            send_sem=fold_send.at[piece],
+            recv_sem=fold_recv.at[piece],
+            device_id=(chan, jnp.int32(path[leg + 1])),
             device_id_type=MESH,
         )
 
@@ -109,9 +110,9 @@
 
     @pl.when(tm == 4)
     def _():
-        for piece in range(4):
-            for way in range(4):
-                fold_copy(way, piece, 0).start()
+        for piece in FOLD_ORDER:
+            path = next(path for path, pieces in FOLD if piece in pieces)
+            fold_copy(path, piece, 0).start()
 
     load = pltpu.make_async_copy(traces, ext.at[:, pl.ds(0, SEG)], load_sem)
     load.start()
@@ -142,14 +143,14 @@
     load.wait()
     table_load.wait()
 
-    for way, path in enumerate(FOLD):
+    for path, pieces in FOLD:
         for leg in range(1, len(path) - 1):
 
             @pl.when(tm == path[leg])
             def _():
-                for piece in range(4):
-                    fold_copy(way, piece, leg - 1).wait_recv()
-                    fold_copy(way, piece, leg).start()
+                for piece in pieces:
+                    fold_copy(path, piece, leg - 1).wait_recv()
+                    fold_copy(path, piece, leg).start()
 
     @pl.when(direct_in)
     def _():
@@ -157,9 +158,9 @@
 
     @pl.when(tm == 3)
     def _():
-        for way, path in enumerate(FOLD):
-            for piece in range(4):
-                fold_copy(way, piece, len(path) - 2).wait_recv()
+        for path, pieces in FOLD:
+            for piece in pieces:
+                fold_copy(path, piece, len(path) - 2).wait_recv()
 
     for step in range(1, 4):
         pl.semaphore_signal(known.at[3], inc=1, device_id=y_peer(step), device_id_type=MESH)
@@ -231,18 +232,19 @@
 
     lax.fori_loop(0, WIN, transform, 0)
 
-    def c_copy(w, from_y):
+    def c_copy(w, from_y, i):
         return pltpu.make_async_remote_copy(
-            src_ref=rec.at[w, from_y, pl.ds(4, 4)],
-            dst_ref=rec.at[w, from_y, pl.ds(0, 4)],
-            send_sem=c_send.at[w, from_y],
-            recv_sem=c_recv.at[w, from_y],
+            src_ref=rec.at[w, from_y, 4 + i],
+            dst_ref=rec.at[w, from_y, i],
+            send_sem=c_send.at[w, from_y, i],
+            recv_sem=c_recv.at[w, from_y, i],
             device_id=(following, tm),
             device_id_type=MESH,
         )
 
     def forward(w):
-        for from_y in range(4):
+        for turn in (2, 3, 1, 0):
+            from_y = (y + turn) % 4
             for i in range(4):
                 arrival = pltpu.make_async_remote_copy(
                     src_ref=white.at[w, 0],
@@ -258,7 +260,7 @@
                 def _():
                     arrival.wait_recv()
 
-            c_copy(w, from_y).start()
+                c_copy(w, from_y, i).start()
 
     sign = jnp.where(lane < 64, 1.0, -1.0)
 
@@ -271,7 +273,8 @@
 
     def add_window(w):
         for from_y in range(4):
-            c_copy(w, from_y).wait_recv()
+            for i in range(4):
+                c_copy(w, from_y, i).wait_recv()
 
         def one(i, carry):
             @pl.when(w == 0)
@@ -297,7 +300,8 @@
 
     lax.fori_loop(0, WIN, exchange, 0)
     for from_y in range(4):
-        c_copy(WIN - 1, from_y).wait_recv()
+        for i in range(4):
+            c_copy(WIN - 1, from_y, i).wait_recv()
 
     norm = 1.0 / math.sqrt(WINDOWS * BAND)
 
@@ -351,6 +355,12 @@
                 own_copy(i, dy).start()
         return carry
 
+    for step in range(1, 4):
+        pl.semaphore_signal(known.at[4], inc=1, device_id=y_peer(step), device_id_type=MESH)
+        pl.semaphore_signal(known.at[4], inc=1, device_id=x_peer(step), device_id_type=MESH)
+    pl.semaphore_signal(known.at[4], inc=1, device_id=partner, device_id_type=MESH)
+    pl.semaphore_signal(known.at[4], inc=1, device_id=sibling, device_id_type=MESH)
+    pl.semaphore_wait(known.at[4], 8)
     lax.fori_loop(0, 4, give, 0)
 
     def take(m, carry):
@@ -379,13 +389,13 @@
     def _():
         halo.wait_send()
 
-    for way, path in enumerate(FOLD):
+    for path, pieces in FOLD:
         for leg in range(len(path) - 1):
 
             @pl.when(tm == path[leg])
             def _():
-                for piece in range(4):
-                    fold_copy(way, piece, leg).wait_send()
+                for piece in pieces:
+                    fold_copy(path, piece, leg).wait_send()
 
     def b_left(w, carry):
         for dx in range(4):
@@ -398,7 +408,8 @@
                 else:
                     b_copy(w, dx, dy).wait_send()
         for from_y in range(4):
-            c_copy(w, from_y).wait_send()
+            for i in range(4):
+                c_copy(w, from_y, i).wait_send()
         return carry
 
     lax.fori_loop(0, WIN, b_left, 0)
@@ -443,10 +454,10 @@
             pltpu.VMEM((4, 4) + piece, jnp.bfloat16),
             pltpu.VMEM((NB,) + piece, jnp.float32),
             pltpu.VMEM((NB,) + piece, jnp.bfloat16),
-            pltpu.VMEM((4, 8, NFFT), jnp.float32),
-            dma, dma, dma, dma, dma((4, 4)), dma((4, 4)),
-            dma((WIN, 16)), dma((WIN, 4, 4)), dma((WIN, 4)), dma((WIN, 4)), dma((2, 4, 4)), dma((2, NB)),
-            pltpu.SemaphoreType.REGULAR((4,)),
+            pltpu.VMEM((16, 8, NFFT), jnp.float32),
+            dma, dma, dma, dma, dma((16,)), dma((16,)),
+            dma((WIN, 16)), dma((WIN, 4, 4)), dma((WIN, 4, 4)), dma((WIN, 4, 4)), dma((2, 4, 4)), dma((2, NB)),
+            pltpu.SemaphoreType.REGULAR((5,)),
         ],
         compiler_params=pltpu.CompilerParams(
             collective_id=0, has_side_effects=True, vmem_limit_bytes=60 * 1024 * 1024

time: 109 us -> 107 us (0.982)
  the two profiles are of different devices: /device:TPU:129 before, /device:TPU:65 now
where the time goes in v3:
time: 107 us; the launch traced here: 105 us
  Pallas kernels  103 us (96%)
  local copies, waits for them, and re-layouts  2.29 us (2%)
    pallas_call x1, Pallas kernels, per_device(): pl.pallas_call(kernel, out_shape=jax.ShapeDtypeStruct((ROUNDS, 2 * NB, 16...  103 us
    unnamed x1, local copies, waits for them, and re-layouts  2.29 us

profile of v3, /device:TPU:65, one launch (start us, length us, event | category | flops | bytes accessed | tf_op | source)
XLA Modules:
  0.0 105.4 jit_solution(8069040122613322387)
XLA Ops:
  0.0 103.1 %shard_map.37 = f32[4,32,16,128]{3,2,1,0:T(8,128)} custom-call(f32[128,4096]{1,0:T(8,128)} %traces.1, s32[4]{0:T(128)} %offsets.1, bf16[2,2,1024,1024]{3,2,1,0:T(8,128)(2,1)} %constant.2.clone.tables), custom_call_target="tpu_custom_call" | custom-call | flops 8000000000 | bytes 16000000 | tf_op jit(solution)/shard_map/pallas_call | solution.py:436
  103.1 2.3 %copy.5 = f32[4,32,16,128]{3,2,1,0:T(8,128)} copy(f32[4,32,16,128]{3,2,1,0:T(8,128)} %shard_map.37) | data formatting | bytes 2097152

commit v4 on v3

--- a/solution.py
+++ b/solution.py
@@ -74,12 +74,11 @@
     for step in range(1, 4):
         pl.semaphore_signal(barrier, inc=1, device_id=x_peer(step), device_id_type=MESH)
         pl.semaphore_signal(barrier, inc=1, device_id=y_peer(step), device_id_type=MESH)
-    pl.semaphore_signal(barrier, inc=1, device_id=sibling, device_id_type=MESH)
     pl.semaphore_signal(barrier, inc=1, device_id=partner, device_id_type=MESH)
     pl.semaphore_signal(barrier, inc=1, device_id=(following, tm), device_id_type=MESH)
     pl.semaphore_signal(barrier, inc=1, device_id=(preceding, tm), device_id_type=MESH)
 
-    pl.semaphore_wait(barrier, 10)
+    pl.semaphore_wait(barrier, 9)
 
     halo = pltpu.make_async_remote_copy(
         src_ref=traces.at[:, pl.ds(0, NFFT)],
@@ -437,9 +436,9 @@
         kernel,
         out_shape=jax.ShapeDtypeStruct((ROUNDS, 2 * NB, 16, CH), jnp.float32),
         in_specs=[
-            pl.BlockSpec(memory_space=pl.ANY),
+            pl.BlockSpec(memory_space=pltpu.HBM),
             pl.BlockSpec(memory_space=pltpu.SMEM),
-            pl.BlockSpec(memory_space=pl.ANY),
+            pl.BlockSpec(memory_space=pltpu.HBM),
         ],
         out_specs=pl.BlockSpec(memory_space=pltpu.VMEM),
         scratch_shapes=[
@@ -460,7 +459,7 @@
             pltpu.SemaphoreType.REGULAR((5,)),
         ],
         compiler_params=pltpu.CompilerParams(
-            collective_id=0, has_side_effects=True, vmem_limit_bytes=60 * 1024 * 1024
+            collective_id=0, has_side_effects=True, vmem_limit_bytes=48 * 1024 * 1024
         ),
         cost_estimate=pl.CostEstimate(flops=8_000_000_000, bytes_accessed=16_000_000, transcendentals=1_000_000),
     )(traces, offsets, tables)

time: 107 us -> 106 us (level)
    pallas_call x1, Pallas kernels: 103 us -> 102 us  [per_device(): pl.pallas_call(kernel, out_shape=jax.ShapeDtypeStruct((ROUNDS, 2 * NB, 16...]
    unnamed x1 -> x5, local copies, waits for them, and re-layouts: 2.29 us -> 3.22 us
where the time goes in v4:
time: 106 us; the launch traced here: 105 us
  Pallas kernels  102 us (96%)
  local copies, waits for them, and re-layouts  3.22 us (3%)
    pallas_call x1, Pallas kernels, per_device(): pl.pallas_call(kernel, out_shape=jax.ShapeDtypeStruct((ROUNDS, 2 * NB, 16...  102 us
    unnamed x5, local copies, waits for them, and re-layouts  3.22 us

profile of v4, /device:TPU:65, one launch (start us, length us, event | category | flops | bytes accessed | tf_op | source)
XLA Modules:
  0.0 105.1 jit_solution(9343634694751521218)
XLA Ops:
  0.0 0.0 copy-start
  0.0 1.6 %copy-done = f32[128,4096]{1,0:T(8,128)S(1)} copy-done((f32[128,4096]{1,0:T(8,128)S(1)}, f32[128,4096]{1,0:T(8,128)}, u32[]{:S(2)}) %copy-start) | copy-done | bytes 2097176
  1.6 0.0 copy-start.1
  1.6 0.7 copy-done.1
  2.2 101.9 %shard_map.37 = f32[4,32,16,128]{3,2,1,0:T(8,128)S(1)} custom-call(f32[128,4096]{1,0:T(8,128)S(1)} %copy-done, s32[4]{0:T(128)S(1)} %copy-done.1, bf16[2,2,1024,1024]{3,2,1,0:T(8,128)(2,1)} %constant.2.clone.tables), custom_call_target="tpu_custom_call" | custom-call | flops 8000000000 | bytes 16000000 | tf_op jit(solution)/shard_map/pallas_call | solution.py:435
  104.1 1.0 copy.5
Async XLA Ops:
  0.0 1.6 %copy-start = (f32[128,4096]{1,0:T(8,128)S(1)}, f32[128,4096]{1,0:T(8,128)}, u32[]{:S(2)}) copy-start(f32[128,4096]{1,0:T(8,128)} %traces.1) | copy-start | bytes 6291460
  1.6 0.7 copy-start.1

commit v5 on v4

--- a/solution.py
+++ b/solution.py
@@ -48,9 +48,9 @@
 
 
 def kernel(
-    traces, offsets, tables, out,
-    ext, tab, turns, split, white, rec, acc, own_out, far_out, own_in, far_in,
-    relay, load_sem, tab_sem, halo_send, halo_recv, fold_send, fold_recv, b_send, b_recv, c_send, c_recv, d_send, d_recv, known,
+    traces, offsets_in, tables, out,
+    offsets, ext, tab, turns, split, white, rec, acc, own_out, far_out, own_in, far_in,
+    relay, offset_sem, load_sem, tab_sem, halo_send, halo_recv, fold_send, fold_recv, b_send, b_recv, c_send, c_recv, d_send, d_recv, known,
 ):
     chan, tm = lax.axis_index("chan"), lax.axis_index("tm")
     zl, x, core = chan // 8, chan // 2 % 4, chan % 2
@@ -115,6 +115,8 @@
 
     load = pltpu.make_async_copy(traces, ext.at[:, pl.ds(0, SEG)], load_sem)
     load.start()
+    offset_load = pltpu.make_async_copy(offsets_in, offsets, offset_sem)
+    offset_load.start()
     table_load = pltpu.make_async_copy(tables, tab, tab_sem)
     table_load.start()
 
@@ -134,6 +136,7 @@
     row = lax.broadcasted_iota(jnp.int32, (NB, 128), 0)
     swapped = row // 8
     frequency = row * BAND + 2 * (column % 32) + (column // 32 + swapped) % 2
+    offset_load.wait()
     for w in range(WIN):
         angle = (frequency * offsets[w] % NFFT).astype(jnp.float32) * (2.0 * math.pi / NFFT)
         turns[w, 0] = jnp.cos(angle)
@@ -356,10 +359,9 @@
 
     for step in range(1, 4):
         pl.semaphore_signal(known.at[4], inc=1, device_id=y_peer(step), device_id_type=MESH)
-        pl.semaphore_signal(known.at[4], inc=1, device_id=x_peer(step), device_id_type=MESH)
     pl.semaphore_signal(known.at[4], inc=1, device_id=partner, device_id_type=MESH)
     pl.semaphore_signal(known.at[4], inc=1, device_id=sibling, device_id_type=MESH)
-    pl.semaphore_wait(known.at[4], 8)
+    pl.semaphore_wait(known.at[4], 5)
     lax.fori_loop(0, 4, give, 0)
 
     def take(m, carry):
@@ -437,11 +439,12 @@
         out_shape=jax.ShapeDtypeStruct((ROUNDS, 2 * NB, 16, CH), jnp.float32),
         in_specs=[
             pl.BlockSpec(memory_space=pltpu.HBM),
-            pl.BlockSpec(memory_space=pltpu.SMEM),
+            pl.BlockSpec(memory_space=pltpu.HBM),
             pl.BlockSpec(memory_space=pltpu.HBM),
         ],
         out_specs=pl.BlockSpec(memory_space=pltpu.VMEM),
         scratch_shapes=[
+            pltpu.SMEM((WIN,), jnp.int32),
             pltpu.VMEM((CH, SEG + NFFT), jnp.float32),
             pltpu.VMEM((2, 2, HALF, HALF), jnp.bfloat16),
             pltpu.VMEM((WIN, 2, NB, 128), jnp.float32),
@@ -454,7 +457,7 @@
             pltpu.VMEM((NB,) + piece, jnp.float32),
             pltpu.VMEM((NB,) + piece, jnp.bfloat16),
             pltpu.VMEM((16, 8, NFFT), jnp.float32),
-            dma, dma, dma, dma, dma((16,)), dma((16,)),
+            dma, dma, dma, dma, dma, dma((16,)), dma((16,)),
             dma((WIN, 16)), dma((WIN, 4, 4)), dma((WIN, 4, 4)), dma((WIN, 4, 4)), dma((2, 4, 4)), dma((2, NB)),
             pltpu.SemaphoreType.REGULAR((5,)),
         ],

time: 106 us -> 114 us (1.075)
  Pallas kernels: 102 us -> 110 us
    pallas_call x1, Pallas kernels: 102 us -> 110 us  [per_device(): pl.pallas_call(kernel, out_shape=jax.ShapeDtypeStruct((ROUNDS, 2 * NB, 16...]
where the time goes in v5:
time: 114 us
  Pallas kernels  110 us (96%)
  local copies, waits for them, and re-layouts  3.22 us (3%)
    pallas_call x1, Pallas kernels, per_device(): pl.pallas_call(kernel, out_shape=jax.ShapeDtypeStruct((ROUNDS, 2 * NB, 16...  110 us
    unnamed x5, local copies, waits for them, and re-layouts  3.22 us

profile of v5, /device:TPU:65, one launch (start us, length us, event | category | flops | bytes accessed | tf_op | source)
XLA Modules:
  0.0 113.6 jit_solution(12906397674871361324)
XLA Ops:
  0.0 0.0 copy-start
  0.0 1.6 %copy-done = f32[128,4096]{1,0:T(8,128)S(1)} copy-done((f32[128,4096]{1,0:T(8,128)S(1)}, f32[128,4096]{1,0:T(8,128)}, u32[]{:S(2)}) %copy-start) | copy-done | bytes 2097176
  1.6 0.0 copy-start.1
  1.6 0.7 copy-done.1
  2.2 110.3 %shard_map.37 = f32[4,32,16,128]{3,2,1,0:T(8,128)S(1)} custom-call(f32[128,4096]{1,0:T(8,128)S(1)} %copy-done, s32[4]{0:T(128)S(1)} %copy-done.1, bf16[2,2,1024,1024]{3,2,1,0:T(8,128)(2,1)} %constant.2.clone.tables), custom_call_target="tpu_custom_call" | custom-call | flops 8000000000 | bytes 16000000 | tf_op jit(solution)/shard_map/pallas_call | solution.py:437
  112.6 1.0 copy.5
Async XLA Ops:
  0.0 1.6 %copy-start = (f32[128,4096]{1,0:T(8,128)S(1)}, f32[128,4096]{1,0:T(8,128)}, u32[]{:S(2)}) copy-start(f32[128,4096]{1,0:T(8,128)} %traces.1) | copy-start | bytes 6291460
  1.6 0.7 copy-start.1
